TPU v7x, 128 devices: a whole 4x4x4 slice. The times are simulated.
128 devices in a mesh: layer: 32 (over z, x, core), dp: 4 (over y).
Axes of the slice: x: 4, y: 4, z: 4, core: 2. Of those that a mesh axis runs over, the one named last changes fastest.
Arguments:
- images: float32 [4, 56, 56, 128], P('dp'), may hold values from -6 to 6
- kernels: bfloat16 [96, 1152, 128], P('layer'), may hold values from -0.1875 to 0.1875
- damping: float32 [96, 128], P('layer'), may hold values from 0.02 to 4
- cotangent: float32 [4, 56, 56, 128], P('dp'), may hold values from -6 to 6
Outputs:
- slab_ends: float32 [32, 4, 56, 56, 128], P('layer', 'dp')
- coarse_ends: float32 [32, 4, 56, 56, 128], P('layer', 'dp')
- adjoint_starts: float32 [32, 4, 56, 56, 128], P('layer', 'dp')
- adjoint_coarse_starts: float32 [32, 4, 56, 56, 128], P('layer', 'dp')
- gradients: float32 [96, 1152, 128], P('layer')
All inputs are finite; a program needn't handle non-finite values.
Results may differ from a plain program's by a relative error of at most 0.0054.
Values sent between devices are 32-bit elements; how exact they have to be, the bound alone decides.
A program may use at most 256 MiB of HBM per device.

v0:
```python
import jax
import jax.numpy as jnp
from jax import lax
from jax.sharding import PartitionSpec as P

STEP = 0.125


def from_behind(shard, axis, by):
    devices = lax.axis_size(axis)
    pairs = [(i, i + by) for i in range(devices) if 0 <= i + by < devices]
    return lax.ppermute(shard, axis, pairs)


def patches(field):
    side = field.shape[1]
    padded = jnp.pad(field, ((0, 0), (1, 1), (1, 1), (0, 0)))
    pieces = [
        padded[:, row_off : row_off + side, col_off : col_off + side, :]
        for row_off in range(3)
        for col_off in range(3)
    ]
    return jnp.concatenate(pieces, axis=-1).reshape(-1, 9 * field.shape[3])


def advance(current, kernel, decay):
    columns = patches(current.astype(jnp.bfloat16))
    preact = jnp.dot(columns, kernel, preferred_element_type=jnp.float32).reshape(current.shape)
    activation = jnp.tanh(preact)
    return (current + STEP * (activation - decay * current), activation, columns)


def retreat(adjoint, activation, kernel_back, decay):
    scaled = (STEP * (1.0 - activation * activation) * adjoint).astype(jnp.bfloat16)
    back_term = jnp.dot(patches(scaled), kernel_back, preferred_element_type=jnp.float32).reshape(
        adjoint.shape
    )
    return (adjoint - STEP * decay * adjoint + back_term, scaled)


def flipped(kernel):
    channels = kernel.shape[1]
    blocks = kernel.reshape(9, channels, channels)[::-1]
    return jnp.swapaxes(blocks, 1, 2).reshape(9 * channels, channels)


def coarse(kernel, decay, layers):
    channels = kernel.shape[1]
    tap_sum = jnp.sum(kernel.astype(jnp.float32).reshape(9, channels, channels), axis=0)
    return jnp.diag(1.0 - layers * STEP * decay) + layers * STEP * tap_sum


def high_dot(left, right):
    return jnp.dot(left, right, precision=lax.Precision.HIGHEST, preferred_element_type=jnp.float32)


def transform(current, matrix):
    return high_dot(current.reshape(-1, matrix.shape[0]), matrix).reshape(current.shape)


def sweep(current, kernel_set, decay_set):
    for layer_id in range(kernel_set.shape[0]):
        current, _, _ = advance(current, kernel_set[layer_id], decay_set[layer_id])
    return current


def sweep_back(adjoint, act_list, back_list, decay_set):
    for layer_id in reversed(range(len(act_list))):
        adjoint, _ = retreat(adjoint, act_list[layer_id], back_list[layer_id], decay_set[layer_id])
    return adjoint


def relay_chain(seed, offset, matrix, backward):
    full_shape = seed.shape
    channels = full_shape[-1]
    seed_rows = seed.reshape(-1, channels)
    term_rows = offset.reshape(-1, channels)
    pieces = 16
    piece_rows = seed_rows.shape[0] // pieces
    span_size = lax.axis_size("layer")
    position = lax.axis_index("layer")
    order_pos = span_size - 1 - position if backward else position

    def advance_block(step_id, state_pair):
        outgoing, collected = state_pair
        if backward:
            incoming = from_behind(outgoing, "layer", -1)
        else:
            incoming = from_behind(outgoing, "layer", 1)
        block_id = step_id - order_pos
        inside = (block_id >= 0) & (block_id < pieces)
        first_row = jnp.clip(block_id, 0, pieces - 1) * piece_rows
        own_rows = lax.dynamic_slice_in_dim(seed_rows, first_row, piece_rows, 0)
        entering = jnp.where(order_pos == 0, own_rows, incoming)
        leaving = high_dot(entering, matrix) + lax.dynamic_slice_in_dim(
            term_rows, first_row, piece_rows, 0
        )
        old_rows = lax.dynamic_slice_in_dim(collected, first_row, piece_rows, 0)
        collected = lax.dynamic_update_slice_in_dim(
            collected, jnp.where(inside, entering, old_rows), first_row, 0
        )
        return (leaving, collected)

    initial = (jnp.zeros((piece_rows, channels), jnp.float32), jnp.zeros_like(seed_rows))
    _, collected = lax.fori_loop(0, span_size + pieces - 1, advance_block, initial)
    return collected.reshape(full_shape)


def coarse_chain(seed, offset, matrix, backward):
    return relay_chain(seed, offset, matrix, backward)


def per_device(images, kernels, damping, cotangent):
    slab = kernels.shape[0]
    channels = images.shape[3]
    span_size = lax.axis_size("layer")
    position = lax.axis_index("layer")
    back_list = [flipped(kernels[layer_id]) for layer_id in range(slab)]
    matrix = coarse(kernels[0], damping[0], slab)
    slab_end = sweep(images, kernels, damping)
    arriving = from_behind(slab_end, "layer", 1)
    start_states = jnp.where(position == 0, images, arriving)
    offset = sweep(start_states, kernels, damping) - transform(start_states, matrix)
    begins = coarse_chain(images, offset, matrix, False)
    coarse_out = transform(begins, matrix) + offset
    current = begins
    act_list = []
    column_list = []
    for layer_id in range(slab):
        current, activation, columns = advance(current, kernels[layer_id], damping[layer_id])
        act_list.append(activation)
        column_list.append(columns)
    head_states = sweep_back(cotangent, act_list, back_list, damping)
    arriving_back = from_behind(head_states, "layer", -1)
    top_states = jnp.where(position == span_size - 1, cotangent, arriving_back)
    back_offset = sweep_back(top_states, act_list, back_list, damping) - transform(
        top_states, matrix.T
    )
    adjoint_state = coarse_chain(cotangent, back_offset, matrix.T, True)
    adjoint_out = transform(adjoint_state, matrix.T) + back_offset
    grad_list = [None] * slab
    for layer_id in reversed(range(slab)):
        adjoint_state, scaled = retreat(
            adjoint_state, act_list[layer_id], back_list[layer_id], damping[layer_id]
        )
        local_grad = lax.dot_general(
            column_list[layer_id],
            scaled.reshape(-1, channels),
            (((0,), (0,)), ((), ())),
            preferred_element_type=jnp.float32,
        )
        local_grad = lax.psum(local_grad, "dp")
        grad_list[layer_id] = local_grad
    stacked = jnp.stack(grad_list)
    return (current[None], coarse_out[None], adjoint_state[None], adjoint_out[None], stacked)


def solution(mesh):
    in_specs = (
        P("dp", None, None, None),
        P("layer", None, None),
        P("layer", None),
        P("dp", None, None, None),
    )
    out_specs = (
        P("layer", "dp", None, None, None),
        P("layer", "dp", None, None, None),
        P("layer", "dp", None, None, None),
        P("layer", "dp", None, None, None),
        P("layer", None, None),
    )
    return jax.shard_map(
        per_device, mesh=mesh, in_specs=in_specs, out_specs=out_specs, check_vma=False
    )
```

profile of v0, /device:TPU:1, one launch (start us, length us, event | category | flops | bytes accessed | tf_op | source)
XLA Modules:
  0.0 1324.5 jit_solution(1375624829719160173)
XLA Ops:
  40.6 8.6 collective-permute-done.2
  62.1 13.1 slice_dynamic-update-slice_fusion.52
  82.0 519.6 %while.34 = (s32[]{:T(128)}, f32[196,128]{1,0:T(8,128)}, f32[3136,128]{1,0:T(8,128)S(1)}, pred[]{:T(512)}, s32[]{:T(128)}, /*index=5*/f32[3136,128]{1,0:T(8,128)...) while((s32[]{:T(128)}, f32[196,128]{1,0:T(8,128)}, ...), condition=%wide.region_2.3_spmd.clone, body=%wide.region_1.2_spmd.clone.sunk | while | flops 38660616 | bytes 1676585 | solution.py:105
  198.8 6.4 collective-permute-start
  210.5 6.4 collective-permute-start
  222.3 6.4 collective-permute-start
  234.0 6.4 collective-permute-start
  245.8 6.5 collective-permute-start
  257.2 6.7 collective-permute-start
  268.9 6.5 collective-permute-start
  280.4 6.7 collective-permute-start
  292.1 6.5 collective-permute-start
  303.6 6.7 collective-permute-start
  315.3 6.5 collective-permute-start
  326.8 6.7 collective-permute-start
  338.5 6.4 collective-permute-start
  350.0 6.7 collective-permute-start
  361.7 6.4 collective-permute-start
  373.2 6.7 collective-permute-start
  384.9 6.4 collective-permute-start
  396.4 6.7 collective-permute-start
  408.1 6.4 collective-permute-start
  419.6 6.4 collective-permute-start
  431.0 6.4 collective-permute-start
  442.4 6.4 collective-permute-start
  453.9 6.4 collective-permute-start
  465.3 6.4 collective-permute-start
  476.8 6.4 collective-permute-start
  488.2 6.4 collective-permute-start
  499.6 6.4 collective-permute-start
  511.1 6.4 collective-permute-start
  522.5 6.4 collective-permute-start
  534.0 6.4 collective-permute-start
  545.4 6.4 collective-permute-start
  556.8 6.4 collective-permute-start
  568.3 6.4 collective-permute-start
  579.7 6.4 collective-permute-start
  591.1 6.4 collective-permute-start
  680.3 525.4 %while.35 = (s32[]{:T(128)}, f32[196,128]{1,0:T(8,128)S(1)}, f32[3136,128]{1,0:T(8,128)S(1)}, pred[]{:T(512)}, s32[]{:T(128)}, /*index=5*/f32[3136,128]{1,0:T(8,...) while((s32[]{:T(128)}, f32[196,128]{1,0:T(8,128)S(1)}, ...), condition=%wide.region_4.5_spmd.clone, body=%wide.region_3.4_spmd.clone.sunk | while | flops 38660616 | bytes 1677096 | solution.py:105
  691.4 8.8 collective-permute-done.1
  714.4 8.8 collective-permute-done.1
  737.3 8.8 collective-permute-done.1
  1098.2 6.2 collective-permute-done.1
  1120.6 6.2 collective-permute-done.1
  1143.0 6.2 collective-permute-done.1
  1165.4 6.2 collective-permute-done.1
  1244.7 6.5 fusion.51
  1251.2 63.3 %all-reduce.21.cloned.1.call-done = (f32[1,1152,128]{2,1,0:T(8,128)}, f32[1,1152,128]{2,1,0:T(8,128)}, f32[1,1152,128]{2,1,0:T(8,128)}) async-done(((f32[1,1152,128]{2,1,0:T(8,128)}, f32[1,1152,128]{2,1,0:T(8,128)}, f32[1,1152,128]{2,1,0:T(8,128)}), (f32[1,1152,128]{2,1,0:T(8,128)}, f32[1,1152,128]{2,1,0:T(8,128)}, f32[1,1152,128]{2,1,0:T(8,128)})) %all-reduce.21.cloned.1.call-update) | async-done | bytes 1769488 | tf_op jit(solution)/shard_map/psum | solution.py:152
  (836 shorter events, 934.1 us)
Async XLA Ops:
  7.2 1307.4 %all-reduce.21.cloned.1.call-start = ((), (), s32[]{:S(2)}) async-start(), calls=%async_computation | async-start | bytes 3538944 | tf_op jit(solution)/shard_map/psum | solution.py:152
  26.7 22.5 %collective-permute-start.2 = (f32[1,56,56,128]{3,2,1,0:T(8,128)}, f32[1,56,56,128]{3,2,1,0:T(8,128)}, u32[]{:S(2)}, u32[]{:S(2)}) collective-permute-start(f32[1,56,56,128]{3,2,1,0:T(8,128)} %fusion.69), channel_id=1, source_target_pairs={{0,4},{4,8},{8,12},{12,16},{16,20},{20,24},{24,28},{28,32},{32,36}... | collective-permute-start | bytes 4816904 | tf_op jit(solution)/shard_map/ppermute | solution.py:12
  198.8 8.1 collective-permute-start
  222.3 8.1 collective-permute-start
  245.8 8.1 collective-permute-start
  257.2 8.3 collective-permute-start
  268.9 8.1 collective-permute-start
  280.4 8.3 collective-permute-start
  292.1 8.1 collective-permute-start
  303.6 8.4 collective-permute-start
  315.3 8.1 collective-permute-start
  326.8 8.4 collective-permute-start
  338.5 8.1 collective-permute-start
  350.0 8.4 collective-permute-start
  361.7 8.1 collective-permute-start
  373.2 8.4 collective-permute-start
  384.9 8.1 collective-permute-start
  396.4 8.4 collective-permute-start
  419.6 8.1 collective-permute-start
  465.3 8.1 collective-permute-start
  511.1 8.1 collective-permute-start
  556.8 8.1 collective-permute-start
  636.1 24.9 %collective-permute-start.3 = (f32[1,56,56,128]{3,2,1,0:T(8,128)S(1)}, f32[1,56,56,128]{3,2,1,0:T(8,128)S(1)}, u32[]{:S(2)}, u32[]{:S(2)}) collective-permute-start(f32[1,56,56,128]{3,2,1,0:T(8,128)S(1)} %fusion.43), channel_id=1, source_target_pairs={{4,0},{8,4},{12,8},{16,12},{20,16},{24,20},{28,24},{32,28},{36,32}... | collective-permute-start | bytes 4816904 | tf_op jit(solution)/shard_map/ppermute | solution.py:12
  689.5 10.7 collective-permute-start.1
  712.4 10.7 collective-permute-start.1
  735.3 10.7 collective-permute-start.1
  749.2 8.1 collective-permute-start.1
  771.6 8.1 collective-permute-start.1
  794.0 8.1 collective-permute-start.1
  816.3 8.1 collective-permute-start.1
  838.7 8.1 collective-permute-start.1
  861.1 8.1 collective-permute-start.1
  883.5 8.1 collective-permute-start.1
  905.9 8.1 collective-permute-start.1
  928.3 8.1 collective-permute-start.1
  950.7 8.1 collective-permute-start.1
  973.1 8.1 collective-permute-start.1
  995.5 8.1 collective-permute-start.1
  1017.9 8.1 collective-permute-start.1
  1029.1 8.1 collective-permute-start.1
  1051.5 8.1 collective-permute-start.1
  1062.7 8.1 collective-permute-start.1
  1073.9 8.1 collective-permute-start.1
  1096.3 8.1 collective-permute-start.1
  1118.7 8.1 collective-permute-start.1
  1141.1 8.1 collective-permute-start.1
  1163.5 8.1 collective-permute-start.1
  1194.8 8.1 collective-permute-start.1
  (82 other events, 643.1 us)
Sparse Core Ops, SparseCore 0:
  1236.5 77.9 all-reduce.20
where the time goes:
time: 1340 us; the launch traced here: 1320 us
  waiting for transfers between devices  443 us (33%)
  starting transfers between devices  376 us (28%)
  matrix products  221 us (16%)
  local copies, waits for them, and re-layouts  162 us (12%)
  other arithmetic  102 us (8%)
  between operations  16.1 us (1%)
    ppermute x96, waiting for transfers between devices, from_behind(): return lax.ppermute(shard, axis, pairs)  380 us
    ppermute x96, starting transfers between devices, from_behind(): return lax.ppermute(shard, axis, pairs)  376 us
    dot_general x98, matrix products, high_dot(): jnp.dot(left, right, precision=lax.Precision.HIGHEST, preferred_element_t...  161 us
    unnamed x233, local copies, waits for them, and re-layouts  77.5 us
    dynamic_update_slice x94, local copies, waits for them, and re-layouts, advance_block(): lax.dynamic_update_slice_in_dim(collected, jnp.where(inside, entering, ol...  67.6 us
    psum x1, waiting for transfers between devices, per_device(): local_grad = lax.psum(local_grad, 'dp')  63.3 us
    select_n x94, other arithmetic, advance_block(): jnp.where(inside, entering, old_rows)  44.7 us
    while x94, other arithmetic  42.1 us
  transfers between devices with their start and end apart: 97, of which 97 were waited for; matrix products, arithmetic and copies ran while one was open for 3% of the time, Pallas kernels for 0%

commit v1 on v0

v1 whole, which is shorter than its diff:
```python
import functools

import jax
import jax.numpy as jnp
from jax import lax
from jax.experimental import pallas as pl
from jax.experimental.pallas import tpu as pltpu
from jax.sharding import PartitionSpec as P

STEP = 0.125
F32 = jnp.float32
BF16 = jnp.bfloat16
MESH = pl.DeviceIdType.MESH
VMEM_BYTES = 60 * 1024 * 1024
WIDE = 64
GROUP = 4


def coarse(kernel, decay, layers):
    channels = kernel.shape[1]
    tap_sum = jnp.sum(kernel.astype(F32).reshape(9, channels, channels), axis=0)
    return jnp.diag(1.0 - layers * STEP * decay) + layers * STEP * tap_sum


def split(value):
    high = value.astype(BF16)
    return high, (value - high.astype(F32)).astype(BF16)


def pack_matrix(matrix, transposed):
    high, low = split(matrix)
    if transposed:
        top = jnp.concatenate([high, high], axis=1)
        bottom = jnp.concatenate([low, jnp.zeros_like(low)], axis=1)
    else:
        top = jnp.concatenate([high, low], axis=1)
        bottom = jnp.concatenate([high, jnp.zeros_like(low)], axis=1)
    return jnp.concatenate([top, bottom], axis=0)


def times(rows, packed, transposed):
    channels = rows.shape[1]
    both = jnp.concatenate(split(rows), axis=1)
    dims = (((1,), (1 if transposed else 0,)), ((), ()))
    result = lax.dot_general(both, packed, dims, preferred_element_type=F32)
    return result[:, :channels] + result[:, channels:]


def clear_edges(packed):
    zeros = jnp.zeros(packed.shape[3:], packed.dtype)
    for col in range(3):
        packed[col, 0, 0] = zeros
        packed[col, 1, packed.shape[2] - 1] = zeros


def pack_rows(packed, first, even, odd):
    count, side, channels = even.shape
    fill = jnp.zeros((count, WIDE - side, channels), F32)
    for parity, value in ((1, even), (0, odd)):
        start = first if parity == 1 else first + 1
        wide = jnp.concatenate([value, fill], axis=1)
        for col, shift in ((1, 0), (0, 1), (2, WIDE - 1)):
            moved = wide if shift == 0 else pltpu.roll(wide, shift, 1)
            packed[col, parity, pl.ds(start, count)] = moved.astype(BF16)


def pieces(packed, first, count):
    channels = packed.shape[-1]
    rows = count * packed.shape[3]
    out = []
    for col in range(3):
        for parity, ahead in ((1, 0), (0, 1), (0, 0), (1, 1)):
            out.append(packed[col, parity, pl.ds(first + ahead, count)].reshape(rows, channels))
    return out


OFFSETS = (0, 1, -1, 2)


def fill_weights(weights, kernel, backward):
    channels = weights.shape[1] // 2 if not backward else weights.shape[0] // 2
    zero = jnp.zeros((channels, channels), BF16)
    for col in range(3):
        for place, offset in enumerate(OFFSETS):
            at = pl.ds((col * 4 + place) * channels, channels)
            for row in range(2):
                tap = offset - row + 1
                if 0 <= tap <= 2:
                    index = tap * 3 + col
                    block = kernel(8 - index if backward else index).astype(BF16)
                else:
                    block = zero
                out = pl.ds(row * channels, channels)
                if backward:
                    weights[out, at] = block
                else:
                    weights[at, out] = block


def convolve(packed, weights, first, count, side, backward):
    left = jnp.concatenate(pieces(packed, first, count), axis=1)
    dims = (((1,), (1 if backward else 0,)), ((), ()))
    result = lax.dot_general(left, weights[...], dims, preferred_element_type=F32)
    channels = result.shape[1] // 2
    result = result.reshape(count, WIDE, 2 * channels)[:, :side]
    return result[:, :, :channels], result[:, :, channels:]


def each_group(pairs, body):
    def step(index, carry):
        body(index * GROUP)
        return carry

    lax.fori_loop(0, pairs // GROUP, step, 0)


def pack_field(packed, field):
    def body(first):
        part = field[pl.ds(first, GROUP)]
        pack_rows(packed, first, part[:, 0], part[:, 1])

    each_group(field.shape[0], body)


def tap_of(ref, layer, channels):
    return lambda tap: ref[layer, pl.ds(tap * channels, channels), :]


def run_forward(source, target, packs, weights, kernels, damping, gates=None, kept=None):
    layers = kernels.shape[0]
    pairs, _, side, channels = source.shape
    for layer in range(layers):
        now, later = packs[layer % 2], packs[(layer + 1) % 2]
        fill_weights(weights, tap_of(kernels, layer, channels), False)
        decay = damping[layer, :].reshape(1, 1, channels)
        state = source if layer == 0 else target

        def body(first):
            outs = convolve(now, weights, first, GROUP, side, False)
            nexts = []
            for row in range(2):
                act = jnp.tanh(outs[row])
                if gates is not None:
                    gates[layer, pl.ds(first, GROUP), row] = STEP * (1.0 - act * act)
                current = state[pl.ds(first, GROUP), row]
                moved = current + STEP * (act - decay * current)
                target[pl.ds(first, GROUP), row] = moved
                nexts.append(moved)
            if kept is not None:
                kept[layer, 0, pl.ds(first, GROUP)] = now[1, 1, pl.ds(first, GROUP)]
                kept[layer, 1, pl.ds(first, GROUP)] = now[1, 0, pl.ds(first + 1, GROUP)]
            if layer + 1 < layers:
                pack_rows(later, first, nexts[0], nexts[1])

        each_group(pairs, body)


def pack_scaled(packed, gates, layer, adjoint):
    def body(first):
        at = pl.ds(first, GROUP)
        pack_rows(packed, first, gates[layer, at, 0] * adjoint[at, 0], gates[layer, at, 1] * adjoint[at, 1])

    each_group(adjoint.shape[0], body)


def run_backward(source, target, packs, weights, kernels, damping, gates, grads=None, kept=None):
    layers = kernels.shape[0]
    pairs, _, side, channels = source.shape
    pack_scaled(packs[0], gates, layers - 1, source)
    for turn, layer in enumerate(reversed(range(layers))):
        now, later = packs[turn % 2], packs[(turn + 1) % 2]
        fill_weights(weights, tap_of(kernels, layer, channels), True)
        decay = damping[layer, :].reshape(1, 1, channels)
        state = source if turn == 0 else target

        def body(first):
            at = pl.ds(first, GROUP)
            outs = convolve(now, weights, first, GROUP, side, True)
            nexts = []
            for row in range(2):
                current = state[at, row]
                moved = current - STEP * decay * current + outs[row]
                target[at, row] = moved
                if layer > 0:
                    nexts.append(gates[layer - 1, at, row] * moved)
            if layer > 0:
                pack_rows(later, first, nexts[0], nexts[1])

        each_group(pairs, body)
        if grads is not None:
            gradient(now, kept, layer, grads)


def gradient(packed, kept, layer, grads):
    channels = packed.shape[-1]
    pairs = packed.shape[2] - 1
    left = jnp.concatenate([kept[layer, row].reshape(pairs * WIDE, channels) for row in range(2)], axis=1)
    for col in range(3):
        parts = []
        for parity, ahead in ((1, 0), (0, 1), (0, 0), (1, 1)):
            parts.append(packed[col, parity, pl.ds(ahead, pairs)].reshape(pairs * WIDE, channels))
        out = lax.dot_general(
            left, jnp.concatenate(parts, axis=1), (((0,), (0,)), ((), ())), preferred_element_type=F32
        )

        def block(row, offset):
            place = OFFSETS.index(offset)
            return out[row * channels : (row + 1) * channels, place * channels : (place + 1) * channels]

        for tap in range(3):
            total = block(0, 1 - tap) + block(1, 2 - tap)
            index = tap * 3 + (2 - col)
            grads[layer, pl.ds(index * channels, channels), :] = total


def rows_times(source, packed_matrix, transposed, put):
    pairs, _, side, channels = source.shape

    def body(first):
        at = pl.ds(first, GROUP)
        for row in range(2):
            rows = source[at, row].reshape(GROUP * side, channels)
            put(at, row, times(rows, packed_matrix, transposed).reshape(GROUP, side, channels))

    each_group(pairs, body)


def offsets_kernel(first_ref, images, before, kernels, damp_before, damping, matrix, out, start, pack_a, pack_b, weights):
    packs = (pack_a, pack_b)
    for packed in packs:
        clear_edges(packed)
    pack_field(pack_a, images)
    run_forward(images, start, packs, weights, before, damp_before)
    is_first = first_ref[0] == 1

    def choose(first):
        at = pl.ds(first, GROUP)
        start[at] = jnp.where(is_first, images[at], start[at])

    each_group(images.shape[0], choose)
    pack_field(pack_a, start)
    run_forward(start, out, packs, weights, kernels, damping)
    packed_matrix = pack_matrix(matrix[...], False)

    def put(at, row, value):
        out[at, row] = out[at, row] - value

    rows_times(start, packed_matrix, False, put)


def middle_kernel(
    last_ref, begins, offsets, cotangent, kernels, after, damping, damp_after, matrix,
    slab_end, coarse_end, back_offset, gates, kept,
    gates_after, state, pack_a, pack_b, weights, weights_back,
):
    packs = (pack_a, pack_b)
    for packed in packs:
        clear_edges(packed)
    packed_matrix = pack_matrix(matrix[...], False)
    packed_transposed = pack_matrix(matrix[...], True)

    def put(at, row, value):
        coarse_end[at, row] = value + offsets[at, row]

    rows_times(begins, packed_matrix, False, put)
    pack_field(pack_a, begins)
    run_forward(begins, slab_end, packs, weights, kernels, damping, gates, kept)
    pack_field(pack_a, coarse_end)
    run_forward(coarse_end, state, packs, weights, after, damp_after, gates_after)
    run_backward(cotangent, state, packs, weights_back, after, damp_after, gates_after)
    is_last = last_ref[0] == 1

    def choose(first):
        at = pl.ds(first, GROUP)
        state[at] = jnp.where(is_last, cotangent[at], state[at])

    each_group(begins.shape[0], choose)
    run_backward(state, back_offset, packs, weights_back, kernels, damping, gates)

    def put_back(at, row, value):
        back_offset[at, row] = back_offset[at, row] - value

    rows_times(state, packed_transposed, True, put_back)


def final_kernel(
    tops, back_offset, kernels, damping, matrix, gates, kept,
    start, coarse_start, grads,
    pack_a, pack_b, weights,
):
    packs = (pack_a, pack_b)
    for packed in packs:
        clear_edges(packed)
    packed_transposed = pack_matrix(matrix[...], True)

    def put(at, row, value):
        coarse_start[at, row] = value + back_offset[at, row]

    run_backward(tops, start, packs, weights, kernels, damping, gates, grads, kept)
    rows_times(tops, packed_transposed, True, put)


def in_vmem(count, scalars=0):
    return [pl.BlockSpec(memory_space=pltpu.SMEM)] * scalars + [
        pl.BlockSpec(memory_space=pltpu.VMEM)
    ] * count


def local_call(kernel, outs, scratch, *args, scalars=0, name=None):
    return pl.pallas_call(
        kernel,
        out_shape=outs,
        in_specs=in_vmem(len(args) - scalars, scalars),
        out_specs=tuple(in_vmem(len(outs))),
        scratch_shapes=scratch,
        compiler_params=pltpu.CompilerParams(vmem_limit_bytes=VMEM_BYTES),
        name=name,
    )(*args)


def chain_kernel(
    chips, backward, window, seed, terms, matrices, out,
    partner_terms, composed, inbox, outbox, returned, partner_out, packs,
    pair_send, pair_recv, in_send, in_recv, back_send, back_recv, out_send, out_recv,
):
    me = lax.axis_index("layer")
    chip = me // 2
    core = me % 2
    partner = me + 1 - 2 * core
    half = seed.shape[0] // 2
    lead = 1 if backward else 0
    is_lead = core == lead
    tiles = half // 8

    def start_of(other):
        return pl.multiple_of((other * tiles) // chips * 8, 8)

    barrier = pltpu.get_barrier_semaphore()
    pl.semaphore_signal(barrier, inc=1, device_id={"layer": partner}, device_id_type=MESH)

    def greet(step, carry):
        other = lax.rem(chip + step, chips)
        pl.semaphore_signal(barrier, inc=1, device_id={"layer": other * 2 + core}, device_id_type=MESH)
        return carry

    lax.fori_loop(1, chips, greet, 0)
    pl.semaphore_wait(barrier, chips)

    own_rows = pl.ds(pl.multiple_of(core * half, 8), half)
    other_rows = pl.ds(pl.multiple_of((1 - core) * half, 8), half)
    exchange = pltpu.make_async_remote_copy(
        src_ref=terms.at[other_rows],
        dst_ref=partner_terms,
        send_sem=pair_send,
        recv_sem=pair_recv,
        device_id={"layer": partner},
        device_id_type=MESH,
    )
    exchange.start()

    def prepare(index, carry):
        packs[index] = pack_matrix(matrices[index], backward)
        return carry

    lax.fori_loop(0, 2 * chips, prepare, 0)
    lead_slab = 2 * chip + lead
    next_slab = 2 * chip + 1 - lead
    exchange.wait()

    block = half // 7
    base = pl.multiple_of(core * half, 8)

    def lead_terms(at, own_at):
        return jnp.where(is_lead, terms[own_at], partner_terms[at])

    def compose(index, carry):
        at = pl.ds(pl.multiple_of(index * block, 8), block)
        own_at = pl.ds(pl.multiple_of(base + index * block, 8), block)
        own, theirs = terms[own_at], partner_terms[at]
        led = jnp.where(is_lead, own, theirs)
        following = jnp.where(is_lead, theirs, own)
        composed[at] = times(led, packs[next_slab], backward) + following
        return carry

    lax.fori_loop(0, 7, compose, 0)

    def in_copy(other):
        return pltpu.make_async_remote_copy(
            src_ref=composed.at[pl.ds(start_of(other), window)],
            dst_ref=inbox.at[chip],
            send_sem=in_send.at[other],
            recv_sem=in_recv.at[chip],
            device_id={"layer": other * 2 + core},
            device_id_type=MESH,
        )

    def send_in(step, carry):
        in_copy(lax.rem(chip + step, chips)).start()
        return carry

    lax.fori_loop(1, chips, send_in, 0)
    inbox[chip] = composed[pl.ds(start_of(chip), window)]

    def in_arrival(other):
        return pltpu.make_async_remote_copy(
            src_ref=composed.at[pl.ds(start_of(other), window)],
            dst_ref=inbox.at[other],
            send_sem=in_send.at[other],
            recv_sem=in_recv.at[other],
            device_id={"layer": other * 2 + core},
            device_id_type=MESH,
        )

    def back_copy(other):
        return pltpu.make_async_remote_copy(
            src_ref=outbox.at[other],
            dst_ref=returned.at[chip],
            send_sem=back_send.at[other],
            recv_sem=back_recv.at[chip],
            device_id={"layer": other * 2 + core},
            device_id_type=MESH,
        )

    def back_arrival(other):
        return pltpu.make_async_remote_copy(
            src_ref=outbox.at[other],
            dst_ref=returned.at[other],
            send_sem=back_send.at[other],
            recv_sem=back_recv.at[other],
            device_id={"layer": other * 2 + core},
            device_id_type=MESH,
        )

    def scan(step, rows):
        at = chips - 1 - step if backward else step
        outbox[at] = rows

        @pl.when(at != chip)
        def _():
            back_copy(at).start()
            in_arrival(at).wait_recv()

        rows = times(rows, packs[2 * at + lead], backward)
        return times(rows, packs[2 * at + 1 - lead], backward) + inbox[at]

    seed_at = pl.multiple_of(base + start_of(chip), 8)
    lax.fori_loop(0, chips, scan, seed[pl.ds(seed_at, window)])

    def gather(step, carry):
        other = lax.rem(chip + step, chips)
        back_arrival(other).wait_recv()
        partner_terms_at = pl.ds(start_of(other), window)
        leads[partner_terms_at] = returned[other]
        return carry

    leads = composed

    def drain_in(step, carry):
        in_copy(lax.rem(chip + step, chips)).wait_send()
        return carry

    lax.fori_loop(1, chips, drain_in, 0)
    lax.fori_loop(1, chips, gather, 0)
    leads[pl.ds(start_of(chip), window)] = outbox[chip]

    def finish(index, carry):
        at = pl.ds(pl.multiple_of(index * block, 8), block)
        own_at = pl.ds(pl.multiple_of(base + index * block, 8), block)
        led = leads[at]
        following = times(led, packs[lead_slab], backward) + lead_terms(at, own_at)
        out[own_at] = jnp.where(is_lead, led, following)
        leads[at] = jnp.where(is_lead, following, led)
        return carry

    lax.fori_loop(0, 7, finish, 0)
    hand = pltpu.make_async_remote_copy(
        src_ref=leads,
        dst_ref=partner_out,
        send_sem=out_send,
        recv_sem=out_recv,
        device_id={"layer": partner},
        device_id_type=MESH,
    )
    hand.start()

    def drain_back(step, carry):
        back_copy(lax.rem(chip + step, chips)).wait_send()
        return carry

    lax.fori_loop(1, chips, drain_back, 0)
    hand.wait()
    out[other_rows] = partner_out[...]


def run_chain(seed, terms, matrices, backward):
    slabs = matrices.shape[0]
    chips = slabs // 2
    rows, channels = terms.shape
    half = rows // 2
    window = -(-(half // 8) // chips) * 8
    dma = pltpu.SemaphoreType.DMA
    return pl.pallas_call(
        functools.partial(chain_kernel, chips, backward, window),
        out_shape=jax.ShapeDtypeStruct((rows, channels), F32),
        in_specs=in_vmem(3),
        out_specs=in_vmem(1)[0],
        scratch_shapes=[
            pltpu.VMEM((half, channels), F32),
            pltpu.VMEM((half, channels), F32),
            pltpu.VMEM((chips, window, channels), F32),
            pltpu.VMEM((chips, window, channels), F32),
            pltpu.VMEM((chips, window, channels), F32),
            pltpu.VMEM((half, channels), F32),
            pltpu.VMEM((slabs, 2 * channels, 2 * channels), BF16),
            dma, dma, dma((chips,)), dma((chips,)), dma((chips,)), dma((chips,)), dma, dma,
        ],
        compiler_params=pltpu.CompilerParams(
            vmem_limit_bytes=VMEM_BYTES,
            collective_id=2 if backward else 1,
            has_side_effects=True,
        ),
        name="chain_back" if backward else "chain",
    )(seed, terms, matrices)


def per_device(images, kernels, damping, cotangent):
    slab, _, channels = kernels.shape
    side = images.shape[1]
    slabs = lax.axis_size("layer")
    position = lax.axis_index("layer")
    pairs = side // 2
    field = (pairs, 2, side, channels)
    rows = (side * side, channels)

    ahead = [(i, i + 1) for i in range(slabs - 1)]
    behind = [(i + 1, i) for i in range(slabs - 1)]
    kernels_f32 = kernels.astype(F32)
    before = lax.ppermute(kernels_f32, "layer", ahead)
    damp_before = lax.ppermute(damping, "layer", ahead)
    after = lax.ppermute(kernels_f32, "layer", behind)
    damp_after = lax.ppermute(damping, "layer", behind)
    matrix = coarse(kernels[0], damping[0], slab)
    matrices = lax.all_gather(matrix, "layer")

    is_first = (position == 0).astype(jnp.int32).reshape(1)
    is_last = (position == slabs - 1).astype(jnp.int32).reshape(1)
    packed = [pltpu.VMEM((3, 2, pairs + 1, WIDE, channels), BF16)] * 2
    weights = [pltpu.VMEM((12 * channels, 2 * channels), BF16)]
    weights_back = [pltpu.VMEM((2 * channels, 12 * channels), BF16)]
    state = jax.ShapeDtypeStruct(field, F32)
    image_pairs = images.reshape(field)
    cot_pairs = cotangent.reshape(field)

    (offsets,) = local_call(
        offsets_kernel, (state,), [pltpu.VMEM(field, F32)] + packed + weights,
        is_first, image_pairs, before, kernels, damp_before, damping, matrix,
        scalars=1, name="offsets",
    )
    begins = run_chain(images.reshape(rows), offsets.reshape(rows), matrices, False)
    gates_shape = (slab,) + field
    slab_end, coarse_end, back_offsets, gates, kept = local_call(
        middle_kernel,
        (
            state, state, state,
            jax.ShapeDtypeStruct(gates_shape, F32),
            jax.ShapeDtypeStruct((slab, 2, pairs, WIDE, channels), BF16),
        ),
        [pltpu.VMEM(gates_shape, F32), pltpu.VMEM(field, F32)] + packed + weights + weights_back,
        is_last, begins.reshape(field), offsets, cot_pairs, kernels, after, damping, damp_after, matrix,
        scalars=1, name="middle",
    )
    tops = run_chain(cotangent.reshape(rows), back_offsets.reshape(rows), matrices, True)
    adjoint_start, adjoint_coarse, grads = local_call(
        final_kernel,
        (state, state, jax.ShapeDtypeStruct(kernels.shape, F32)),
        packed + weights_back,
        tops.reshape(field), back_offsets, kernels, damping, matrix, gates, kept,
        name="final",
    )
    grads = lax.psum(grads, "dp")
    full = (1,) + images.shape
    return (
        slab_end.reshape(full),
        coarse_end.reshape(full),
        adjoint_start.reshape(full),
        adjoint_coarse.reshape(full),
        grads,
    )


def solution(mesh):
    in_specs = (
        P("dp", None, None, None),
        P("layer", None, None),
        P("layer", None),
        P("dp", None, None, None),
    )
    out_specs = (
        P("layer", "dp", None, None, None),
        P("layer", "dp", None, None, None),
        P("layer", "dp", None, None, None),
        P("layer", "dp", None, None, None),
        P("layer", None, None),
    )
    return jax.shard_map(
        per_device, mesh=mesh, in_specs=in_specs, out_specs=out_specs, check_vma=False
    )
```

time: 1340 us -> 282 us (0.21); the launches traced: 1320 us -> 282 us
  waiting for transfers between devices: 443 us -> 68.4 us
  starting transfers between devices: 376 us -> 12.1 us
  matrix products: 221 us -> 0 us
  Pallas kernels: 0 us -> 179 us
  local copies, waits for them, and re-layouts: 162 us -> 6.2 us
  other arithmetic: 102 us -> 2.33 us
    ppermute x96 -> x4, waiting for transfers between devices: 380 us -> 12.3 us  [the longest x1 12.3 us: per_device(): damp_before = lax.ppermute(damping, 'layer', ahead)]
    ppermute x96 -> x4, starting transfers between devices: 376 us -> 12 us  [the longest x1 4.51 us: per_device(): before = lax.ppermute(kernels_f32, 'layer', ahead)]
    dot_general x119 -> x0, matrix products: 221 us -> none  [the longest x98 161 us: high_dot(): jnp.dot(left, right, precision=lax.Precision.HIGHEST, preferred_element_t...]
    pallas_call x0 -> x5, Pallas kernels: none -> 179 us  [the longest x3 94.6 us: local_call(): pl.pallas_call(kernel, out_shape=outs, in_specs=in_vmem(len(args) - scala...]
    unnamed x233 -> x15, local copies, waits for them, and re-layouts: 77.5 us -> 5.22 us
    dynamic_update_slice x94 -> x0, local copies, waits for them, and re-layouts: 67.6 us -> none  [advance_block(): lax.dynamic_update_slice_in_dim(collected, jnp.where(inside, entering, ol...]
    select_n x94 -> x0, other arithmetic: 44.7 us -> none  [advance_block(): jnp.where(inside, entering, old_rows)]
    while x94 -> x0, other arithmetic: 42.1 us -> none
  transfers between devices with their start and end apart: 97 -> 6, of which waited for: 97 -> 3; matrix products, arithmetic and copies ran while one was open for 3% -> 0% of each run, Pallas kernels for 0% -> 21%
where the time goes in v1:
time: 282 us
  Pallas kernels  179 us (63%)
  waiting for transfers between devices  68.4 us (24%)
  between operations  14.2 us (5%)
  starting transfers between devices  12.1 us (4%)
  local copies, waits for them, and re-layouts  6.2 us (2%)
    pallas_call x3, Pallas kernels, local_call(): pl.pallas_call(kernel, out_shape=outs, in_specs=in_vmem(len(args) - scala...  94.6 us
    pallas_call x2, Pallas kernels, run_chain(): pl.pallas_call(functools.partial(chain_kernel, chips, backward, window),...  84.1 us
    psum x1, waiting for transfers between devices, per_device(): grads = lax.psum(grads, 'dp')  49.8 us
    ppermute x1, waiting for transfers between devices, per_device(): damp_before = lax.ppermute(damping, 'layer', ahead)  12.3 us
    all_gather x1, waiting for transfers between devices, per_device(): matrices = lax.all_gather(matrix, 'layer')  6.28 us
  transfers between devices with their start and end apart: 6, of which 3 were waited for; matrix products, arithmetic and copies ran while one was open for 0% of the time, Pallas kernels for 21%

profile of v1, /device:TPU:1, one launch (start us, length us, event | category | flops | bytes accessed | tf_op | source)
XLA Modules:
  0.0 281.9 jit_solution(10290039624503451878)
XLA Ops:
  7.2 0.0 copy-start
  7.2 0.0 all-gather.2.cloned.1.call-start
  7.2 0.8 subtract_bitcast_fusion
  8.0 1.0 slice.7
  9.0 0.0 copy-start.4
  9.0 0.0 copy-start.2
  9.0 0.6 copy-done.2
  9.7 0.7 bitcast_add_fusion
  10.4 0.0 all-gather.2.cloned.1.call-update
  10.4 0.0 all-reduce.2.cloned.1.call-start
  10.4 0.0 copy-done
  10.5 0.0 copy-start.3
  10.5 0.1 convert_element_type.16
  10.6 4.5 %collective-permute-start = (f32[3,1152,128]{2,1,0:T(8,128)S(1)}, f32[3,1152,128]{2,1,0:T(8,128)}, u32[]{:S(2)}, u32[]{:S(2)}) collective-permute-start(f32[3,1152,128]{2,1,0:T(8,128)S(1)} %convert_element_type.16), channel_id=1, source_target_pairs={{0,4},{4,8},{8,12},{12,16},{16,20},{20,24},{24,28},{28,32},{32,36}... | collective-permute-start | bytes 5308424 | tf_op jit(solution)/shard_map/ppermute | solution.py:538
  15.1 1.9 collective-permute-start.2
  17.0 0.0 copy-done.4
  17.0 1.9 collective-permute-start.3
  19.0 3.6 %collective-permute-start.1 = (f32[3,128]{1,0:T(4,128)S(1)}, f32[3,128]{1,0:T(4,128)S(1)}, u32[]{:S(2)}, u32[]{:S(2)}) collective-permute-start(f32[3,128]{1,0:T(4,128)S(1)} %copy-done.4), channel_id=1, source_target_pairs={{0,4},{4,8},{8,12},{12,16},{16,20},{20,24},{24,28},{28,32},{32,36}... | collective-permute-start | bytes 4616 | tf_op jit(solution)/shard_map/ppermute | solution.py:539
  22.6 0.0 copy-done.3
  22.6 0.7 select_add_fusion.matrix
  23.3 12.3 %collective-permute-done.1.damp_before = f32[3,128]{1,0:T(4,128)S(1)} collective-permute-done((f32[3,128]{1,0:T(4,128)S(1)}, f32[3,128]{1,0:T(4,128)S(1)}, u32[]{:S(2)}, u32[]{:S(2)}) %collective-permute-start.1) | collective-permute-done | bytes 1568 | tf_op jit(solution)/shard_map/ppermute | solution.py:539
  35.6 0.0 copy-start.6
  35.6 0.0 collective-permute-done.before
  35.6 0.6 copy-done.6
  36.2 23.1 %offsets.1 = f32[28,2,56,128]{3,2,1,0:T(8,128)} custom-call(s32[1]{0:T(128)} %bitcast.2.first_ref, f32[28,2,56,128]{3,2,1,0:T(8,128)} %bitcast.26, f32[3,1152,128]{2,1,0:T(8,128)} %collective-permute-done.before, bf16[3,1152,128]{2,1,0:T(8,128)(2,1)} %kernels.5, f32[3,128]{1,0:T(4,128)} %copy-done.6, f32[3,128]{1,0:T(4,128)} %damping.5, ...), custom_call_target="tpu_custom_call" | custom-call | tf_op jit(solution)/shard_map/offsets/pallas_call | solution.py:310
  59.3 6.3 %all-gather.2.cloned.1.call-done.matrices = f32[32,128,128]{2,1,0:T(8,128)} async-done(((f32[1,128,128]{2,1,0:T(8,128)}), f32[32,128,128]{2,1,0:T(8,128)}) %all-gather.2.cloned.1.call-update) | async-done | bytes 2097168 | tf_op jit(solution)/shard_map/all_gather | solution.py:543
  65.6 35.9 %chain.1 = f32[3136,128]{1,0:T(8,128)} custom-call(f32[3136,128]{1,0:T(8,128)} %bitcast.27, f32[3136,128]{1,0:T(8,128)} %bitcast.20, f32[32,128,128]{2,1,0:T(8,128)} %all-gather.2.cloned.1.call-done.matrices), custom_call_target="tpu_custom_call" | custom-call | tf_op jit(solution)/shard_map/chain/pallas_call | solution.py:502
  101.5 0.0 collective-permute-done.3.damp_after
  101.5 0.0 copy-start.5
  101.6 0.0 collective-permute-done.2.after
  101.6 0.0 copy-start.1
  101.6 0.5 copy-done.5
  102.1 0.7 copy-done.1
  102.8 49.0 %middle.1 = (f32[28,2,56,128]{3,2,1,0:T(8,128)}, f32[28,2,56,128]{3,2,1,0:T(8,128)}, f32[28,2,56,128]{3,2,1,0:T(8,128)}, f32[3,28,2,56,128]{4,3,2,1,0:T(8,128)}, bf16[3,2,28,64,128]{4,3,2,1,0:T(8,128)(2,1)}) custom-call(s32[1]{0:T(128)} %bitcast.last_ref, f32[28,2,56,128]{3,2,1,0:T(8,128)} %bitcast.23, f32[28,2,56,128]{3,2,1,0:T(8,128)} %offsets.1, ...), custom_call_target="tpu_custom_call" | custom-call | tf_op jit(solution)/shard_map/middle/pallas_call | solution.py:310
  151.7 48.2 %chain_back.1 = f32[3136,128]{1,0:T(8,128)} custom-call(f32[3136,128]{1,0:T(8,128)} %bitcast.22, f32[3136,128]{1,0:T(8,128)} %bitcast.24, f32[32,128,128]{2,1,0:T(8,128)} %all-gather.2.cloned.1.call-done.matrices), custom_call_target="tpu_custom_call" | custom-call | tf_op jit(solution)/shard_map/chain_back/pallas_call | solution.py:502
  199.9 22.5 %final.1 = (f32[28,2,56,128]{3,2,1,0:T(8,128)}, f32[28,2,56,128]{3,2,1,0:T(8,128)}, f32[3,1152,128]{2,1,0:T(8,128)}) custom-call(f32[28,2,56,128]{3,2,1,0:T(8,128)} %bitcast.25, f32[28,2,56,128]{3,2,1,0:T(8,128)} %get-tuple-element.15.back_offset, bf16[3,1152,128]{2,1,0:T(8,128)(2,1)} %kernels.5, f32[3,128]{1,0:T(4,128)} %damping.5, ...), custom_call_target="tpu_custom_call" | custom-call | tf_op jit(solution)/shard_map/final/pallas_call | solution.py:310
  222.4 0.0 all-reduce.2.cloned.1.call-update
  222.4 49.8 %all-reduce.2.cloned.1.call-done = f32[3,1152,128]{2,1,0:T(8,128)} async-done(((f32[3,1152,128]{2,1,0:T(8,128)}), f32[3,1152,128]{2,1,0:T(8,128)}) %all-reduce.2.cloned.1.call-update) | async-done | bytes 1769488 | tf_op jit(solution)/shard_map/psum | solution.py:580
  272.3 2.8 copy.10
  (1 shorter events, 0.0 us)
Async XLA Ops:
  7.2 3.3 %copy-start = (bf16[3,1152,128]{2,1,0:T(8,128)(2,1)S(1)}, bf16[3,1152,128]{2,1,0:T(8,128)(2,1)}, u32[]{:S(2)}) copy-start(bf16[3,1152,128]{2,1,0:T(8,128)(2,1)} %kernels.5) | copy-start | bytes 2654212
  7.2 58.4 %all-gather.2.cloned.1.call-start = ((), (), s32[]{:S(2)}) async-start(), calls=%async_computation | async-start | bytes 2162688 | tf_op jit(solution)/shard_map/all_gather | solution.py:543
  9.0 8.1 %copy-start.4 = (f32[3,128]{1,0:T(4,128)S(1)}, f32[3,128]{1,0:T(4,128)}, u32[]{:S(2)}) copy-start(f32[3,128]{1,0:T(4,128)} %damping.5) | copy-start | bytes 4612
  9.0 0.6 copy-start.2
  10.4 261.9 %all-reduce.2.cloned.1.call-start = ((), (), s32[]{:S(2)}) async-start(), calls=%async_computation.1 | async-start | bytes 3538944 | tf_op jit(solution)/shard_map/psum | solution.py:580
  10.5 12.2 %copy-start.3 = (f32[128,128]{1,0:T(8,128)S(1)}, f32[128,128]{1,0:T(8,128)}, u32[]{:S(2)}) copy-start(f32[128,128]{1,0:T(8,128)} %copy-done.2) | copy-start | bytes 196612
  10.6 25.0 %collective-permute-start = (f32[3,1152,128]{2,1,0:T(8,128)S(1)}, f32[3,1152,128]{2,1,0:T(8,128)}, u32[]{:S(2)}, u32[]{:S(2)}) collective-permute-start(f32[3,1152,128]{2,1,0:T(8,128)S(1)} %convert_element_type.16), channel_id=1, source_target_pairs={{0,4},{4,8},{8,12},{12,16},{16,20},{20,24},{24,28},{28,32},{32,36}... | collective-permute-start | bytes 5308424 | tf_op jit(solution)/shard_map/ppermute | solution.py:538
  15.1 86.4 %collective-permute-start.2 = (f32[3,1152,128]{2,1,0:T(8,128)S(1)}, f32[3,1152,128]{2,1,0:T(8,128)S(1)}, u32[]{:S(2)}, u32[]{:S(2)}) collective-permute-start(f32[3,1152,128]{2,1,0:T(8,128)S(1)} %convert_element_type.16), channel_id=1, source_target_pairs={{4,0},{8,4},{12,8},{16,12},{20,16},{24,20},{28,24},{32,28},{36,32}... | collective-permute-start | bytes 5308424 | tf_op jit(solution)/shard_map/ppermute | solution.py:540
  17.0 84.5 %collective-permute-start.3 = (f32[3,128]{1,0:T(4,128)S(1)}, f32[3,128]{1,0:T(4,128)S(1)}, u32[]{:S(2)}, u32[]{:S(2)}) collective-permute-start(f32[3,128]{1,0:T(4,128)S(1)} %copy-done.4), channel_id=1, source_target_pairs={{4,0},{8,4},{12,8},{16,12},{20,16},{24,20},{28,24},{32,28},{36,32}... | collective-permute-start | bytes 4616 | tf_op jit(solution)/shard_map/ppermute | solution.py:541
  19.0 16.7 %collective-permute-start.1 = (f32[3,128]{1,0:T(4,128)S(1)}, f32[3,128]{1,0:T(4,128)S(1)}, u32[]{:S(2)}, u32[]{:S(2)}) collective-permute-start(f32[3,128]{1,0:T(4,128)S(1)} %copy-done.4), channel_id=1, source_target_pairs={{0,4},{4,8},{8,12},{12,16},{16,20},{20,24},{24,28},{28,32},{32,36}... | collective-permute-start | bytes 4616 | tf_op jit(solution)/shard_map/ppermute | solution.py:539
  35.6 0.6 copy-start.6
  101.5 0.6 copy-start.5
  101.6 1.2 copy-start.1
Sparse Core Ops, SparseCore 0:
  10.8 54.6 all-gather.1
  222.6 49.6 all-reduce.1
